TPU v7x, 128 devices: a whole 4x4x4 slice. The times are simulated.
128 devices in a mesh: wide: 8 (over x, y_hi), narrow: 16 (over y_lo, z, core).
Axes of the slice: x: 4, y: 4 (y_hi: 2, y_lo: 2; y = y_hi * 2 + y_lo), z: 4, core: 2. Of those that a mesh axis runs over, the one named last changes fastest.
Arguments:
- tokens: bfloat16 [8192, 4096], P('narrow'), may hold values from -6 to 6
- norm_gain: float32 [4096], replicated, may hold values from 0.1 to 1.9
- coded: bfloat16 [4096, 14336], P('narrow', 'wide'), may hold values from -0.09375 to 0.09375
- block_codes: int32 [32, 112], P('narrow', 'wide'), may hold values from 0 to 15
- grid: float32 [16], replicated, may hold values from 0.5 to 2
- cotangent: bfloat16 [8192, 14336], P('narrow', 'wide'), may hold values from -6 to 6
Outputs:
- activated: bfloat16 [8192, 14336], P('narrow', 'wide')
- weight_grad: float32 [4096, 14336], P('narrow', 'wide')
- input_grad: bfloat16 [8192, 4096], P('narrow', 'wide')
All inputs are finite; a program needn't handle non-finite values.
Results may differ from a plain program's by a relative error of at most 0.017.
Values may be sent and summed in bfloat16 or wider, within the bound.
A program may use at most 128 MiB of HBM per device.

v0:
```python
import jax
import jax.numpy as jnp
from jax import lax
from jax.sharding import Mesh
from jax.sharding import PartitionSpec as P

BLOCK = 128
WIDE = ("wide_0", "wide_1")


def summed_rows(shard, axes, dim):
    if not axes:
        return shard
    nearer = lax.psum_scatter(shard, axes[0], scatter_dimension=dim, tiled=True)
    return summed_rows(nearer, axes[1:], dim)


def copy_for_each(shard, axis):
    length = lax.axis_size(axis)
    return lax.all_to_all(
        jnp.broadcast_to(shard[None], (length, *shard.shape)), axis, 0, 0, tiled=True
    )


def over_copies(shard, axis):
    everything = copy_for_each(shard, axis)
    return jnp.sum(everything, axis=0)


def hadamard(size):
    index = jnp.arange(size, dtype=jnp.int32)
    parity = jnp.zeros((size, size), jnp.int32)
    for level in range(size.bit_length() - 1):
        stride = 2**level
        parity = parity + index[:, None] // stride % 2 * (index[None, :] // stride % 2)
    return (1 - 2 * (parity % 2)).astype(jnp.bfloat16)


def decode(coded, block_codes, grid):
    nrows, ncols = coded.shape
    rotation = hadamard(BLOCK)
    onehot = (
        block_codes[:, :, None] == jnp.arange(grid.shape[0], dtype=jnp.int32)[None, None, :]
    ).astype(jnp.float32)
    block_scale = jnp.sum(onehot * grid[None, None, :], axis=-1) / jnp.sqrt(jnp.float32(BLOCK))
    blocks = coded.reshape(nrows // BLOCK, BLOCK, ncols // BLOCK, BLOCK)

    def one_row(pair):
        piece, scales = pair
        turned = jnp.einsum("ikj,jl->ikl", piece, rotation, preferred_element_type=jnp.float32)
        return (turned * scales[None, :, None]).reshape(BLOCK, ncols).astype(jnp.bfloat16)

    return lax.map(one_row, (blocks, block_scale)).reshape(nrows, ncols)


def per_device(tokens, norm_gain, coded, block_codes, grid, cotangent):
    weight = lax.all_gather(decode(coded, block_codes, grid), "narrow", axis=0, tiled=True)
    inputs = tokens.astype(jnp.float32)
    inv_rms = lax.rsqrt(jnp.mean(inputs * inputs, axis=-1, keepdims=True) + 1e-05)
    normed = (inputs * inv_rms * norm_gain[None, :]).astype(jnp.bfloat16)
    preact = jnp.dot(normed, weight, preferred_element_type=jnp.float32)
    sig = jax.nn.sigmoid(preact)
    activated = (preact * sig).astype(jnp.bfloat16)
    pre_grad = (cotangent.astype(jnp.float32) * sig * (1.0 + preact * (1.0 - sig))).astype(
        jnp.bfloat16
    )
    weight_grad = lax.psum_scatter(
        lax.dot_general(
            normed, pre_grad, (((0,), (0,)), ((), ())), preferred_element_type=jnp.float32
        ).astype(jnp.bfloat16),
        "narrow",
        scatter_dimension=0,
        tiled=True,
    ).astype(jnp.float32)
    partial_value = lax.dot_general(
        pre_grad, weight, (((1,), (1,)), ((), ())), preferred_element_type=jnp.float32
    )
    share = inputs.shape[1] // lax.axis_size(WIDE)
    offset = lax.axis_index(WIDE) * share
    grad_share = summed_rows(partial_value.astype(jnp.bfloat16), WIDE, 1).astype(jnp.float32)
    gain_share = lax.dynamic_slice_in_dim(norm_gain, offset, share, 0)
    input_share = lax.dynamic_slice_in_dim(inputs, offset, share, 1)
    scaled_grad = grad_share * gain_share[None, :]
    local_dot = jnp.sum(scaled_grad * input_share, axis=-1, keepdims=True)
    row_dot = over_copies(local_dot, WIDE) / inputs.shape[1]
    input_grad = (inv_rms * scaled_grad - input_share * inv_rms**3 * row_dot).astype(jnp.bfloat16)
    return (activated, weight_grad, input_grad)


def solution(mesh):
    torus = Mesh(mesh.devices.reshape(4, 2, mesh.shape["narrow"]), ("wide_0", "wide_1", "narrow"))
    placed = (P("narrow", None), P(), P("narrow", WIDE), P("narrow", WIDE), P(), P("narrow", WIDE))
    return jax.shard_map(
        per_device,
        mesh=torus,
        in_specs=placed,
        out_specs=(P("narrow", WIDE), P("narrow", WIDE), P("narrow", WIDE)),
        check_vma=False,
    )
```

profile of v0, /device:TPU:1, one launch (start us, length us, event | category | flops | bytes accessed | tf_op | source)
XLA Modules:
  0.0 300.0 jit_solution(7026429546753846589)
XLA Ops:
  7.2 0.0 all-gather.2.cloned.1.call-start
  7.3 1.8 reshape.713
  9.1 0.2 copy.17
  9.4 0.1 copy.16
  9.5 0.2 fusion.33
  9.6 0.1 copy.18
  9.7 1.4 while.11
  9.7 0.4 fusion.50
  10.1 0.2 copy.25
  10.4 0.4 fusion.50
  10.9 0.2 copy.25
  11.2 0.9 copy-done
  12.1 0.0 all-gather.2.cloned.1.call-update
  12.1 0.0 reduce-scatter.6.cloned.1.call-start
  12.1 3.1 %multiply_reduce_fusion = f32[512]{0:T(512)S(1)} fusion(bf16[512,4096]{1,0:T(8,128)(2,1)} %param.8), kind=kLoop, calls=%fused_computation.38 | loop fusion | flops 6290944 | bytes 4196352 | tf_op jit(solution)/shard_map/reduce_sum | solution.py:59
  15.2 82.4 %all-gather.2.cloned.1.call-done = bf16[4096,1792]{1,0:T(8,128)(2,1)} async-done(((bf16[256,1792]{1,0:T(8,128)(2,1)}), bf16[4096,1792]{1,0:T(8,128)(2,1)}) %all-gather.2.cloned.1.call-update) | async-done | bytes 14680080 | tf_op jit(solution)/shard_map/all_gather | solution.py:57
  97.7 14.8 %multiply_convert_fusion.2 = (bf16[512,1792]{1,0:T(8,128)(2,1)}, f32[512,1792]{1,0:T(8,128)S(1)}) fusion(bf16[4096,1792]{1,0:T(8,128)(2,1)} %all-gather.2.cloned.1.call-done, f32[4096]{0:T(1024)S(1)} %copy-done.3, f32[512]{0:T(512)S(1)} %get-tuple-element.118, bf16[512,4096]{1,0:T(8,128)(2,1)} %param.8), kind=kOutput, calls=%fused_computation.41 | convolution fusion | flops 7529168896 | bytes 24397824 | tf_op jit(solution)/shard_map/dot_general | solution.py:61
  112.4 1.9 copy-done.5
  114.3 14.6 %convolution_convert_fusion.1 = bf16[512,4096]{1,0:T(8,128)(2,1)} fusion(bf16[4096,1792]{1,0:T(8,128)(2,1)} %all-gather.2.cloned.1.call-done, f32[512,1792]{1,0:T(8,128)S(1)} %get-tuple-element.120, bf16[512,1792]{1,0:T(8,128)(2,1)S(1)} %copy-done.4), kind=kOutput, calls=%fused_computation.39 | convolution fusion | flops 7527464960 | bytes 24379392 | tf_op jit(solution)/shard_map/dot_general | solution.py:75
  128.9 0.0 reduce-scatter.6.cloned.1.call-update
  128.9 0.0 reduce-scatter.8.cloned.1.call-start
  128.9 47.5 %reduce-scatter.6.cloned.1.call-done = bf16[512,1024]{1,0:T(8,128)(2,1)} async-done(((bf16[512,4096]{1,0:T(8,128)(2,1)}), bf16[512,1024]{1,0:T(8,128)(2,1)}) %reduce-scatter.6.cloned.1.call-update) | async-done | bytes 1048592 | tf_op jit(solution)/shard_map/reduce_scatter | solution.py:14
  176.4 0.2 reduce-scatter.4.cloned.1.call-start
  176.7 14.2 %convolution_convert_fusion = bf16[4096,1792]{1,0:T(8,128)(2,1)} fusion(f32[4096]{0:T(1024)S(1)} %copy-done.3, f32[512]{0:T(512)S(1)} %get-tuple-element.118, bf16[512,4096]{1,0:T(8,128)(2,1)} %param.8, f32[512,1792]{1,0:T(8,128)} %copy-done.5, bf16[512,1792]{1,0:T(8,128)(2,1)S(1)} %copy-done.4), kind=kOutput, calls=%fused_computation.36 | convolution fusion | flops 7541096448 | bytes 24397824 | tf_op jit(solution)/shard_map/dot_general | solution.py:68
  190.9 6.5 %convert_element_type.47 = f32[512,4096]{1,0:T(8,128)} convert(bf16[512,4096]{1,0:T(8,128)(2,1)} %param.8) | non-fusion elementwise | flops 2097152 | bytes 12582912 | tf_op jit(solution)/shard_map/convert_element_type | solution.py:58
  197.5 0.1 dynamic_slice.14
  197.6 5.4 %reduce-scatter.8.cloned.1.call-done = bf16[512,512]{1,0:T(8,128)(2,1)} async-done(((bf16[512,1024]{1,0:T(8,128)(2,1)}), bf16[512,512]{1,0:T(8,128)(2,1)}) %reduce-scatter.8.cloned.1.call-update) | async-done | bytes 524304 | tf_op jit(solution)/shard_map/reduce_scatter | solution.py:14
  203.0 1.6 multiply_reduce_fusion.1
  204.6 10.3 %all_to_all.5 = f32[8,512,1]{1,2,0:T(1,128)S(1)} all-to-all(f32[8,512,1]{1,2,0:T(1,128)S(1)} %broadcast_in_dim.6), channel_id=1, replica_groups=mesh['wide_0'=4,'wide_1'=2,'narrow'=16] {'wide_0','wide_1'}, dimensions={0} | all-to-all | bytes 32768 | tf_op jit(solution)/shard_map/all_to_all | solution.py:20
  214.9 2.5 subtract_convert_fusion
  217.4 73.5 %reduce-scatter.4.cloned.1.call-done = bf16[256,1792]{1,0:T(8,128)(2,1)} async-done(((bf16[4096,1792]{1,0:T(8,128)(2,1)}), bf16[256,1792]{1,0:T(8,128)(2,1)}) %reduce-scatter.4.cloned.1.call-update) | async-done | bytes 917520 | tf_op jit(solution)/shard_map/reduce_scatter | solution.py:67
  291.0 2.5 convert_element_type.54
  (26 shorter events, 0.2 us)
Async XLA Ops:
  7.2 2.2 copy-start.1
  7.2 2.3 copy-start.2
  7.2 90.5 %all-gather.2.cloned.1.call-start = ((), (), s32[]{:S(2)}) async-start(), calls=%async_computation.4 | async-start | bytes 15597568 | tf_op jit(solution)/shard_map/all_gather | solution.py:57
  11.1 0.9 copy-start
  11.2 86.5 %copy-start.3 = (f32[4096]{0:T(1024)S(1)}, f32[4096]{0:T(1024)}, u32[]{:S(2)}) copy-start(f32[4096]{0:T(1024)} %param.9) | copy-start | bytes 49156
  12.1 164.3 %reduce-scatter.6.cloned.1.call-start = ((), (), s32[]{:S(2)}) async-start(), calls=%async_computation.6 | async-start | bytes 5242880 | tf_op jit(solution)/shard_map/reduce_scatter | solution.py:14
  97.7 16.6 %copy-start.4 = (bf16[512,1792]{1,0:T(8,128)(2,1)S(1)}, bf16[512,1792]{1,0:T(8,128)(2,1)}, u32[]{:S(2)}) copy-start(bf16[512,1792]{1,0:T(8,128)(2,1)} %param.13) | copy-start | bytes 5505028
  112.4 1.9 copy-start.5
  128.9 74.1 %reduce-scatter.8.cloned.1.call-start = ((), (), s32[]{:S(2)}) async-start(), calls=%async_computation.7 | async-start | bytes 1572864 | tf_op jit(solution)/shard_map/reduce_scatter | solution.py:14
  176.4 114.5 %reduce-scatter.4.cloned.1.call-start = ((), (), s32[]{:S(2)}) async-start(), calls=%async_computation.5 | async-start | bytes 15597568 | tf_op jit(solution)/shard_map/reduce_scatter | solution.py:67
Sparse Core Ops, SparseCore 0:
  12.2 85.4 all-gather.1
  129.0 47.3 reduce-scatter.5
  178.9 24.0 reduce-scatter.7
  205.2 85.6 reduce-scatter.3
where the time goes:
time: 301 us; the launch traced here: 300 us
  waiting for transfers between devices  209 us (69%)
  matrix products  44.4 us (15%)
  other arithmetic  16.4 us (5%)
  between operations  13.9 us (5%)
  blocking collectives  10.3 us (3%)
  local copies, waits for them, and re-layouts  5.63 us (2%)
    all_gather x1, waiting for transfers between devices, per_device(): lax.all_gather(decode(coded, block_codes, grid), 'narrow', axis=0, tiled=...  82.4 us
    reduce_scatter x1, waiting for transfers between devices, per_device(): lax.psum_scatter(lax.dot_general(normed, pre_grad, (((0,), (0,)), ((), ()...  73.5 us
    reduce_scatter x2, waiting for transfers between devices, summed_rows(): nearer = lax.psum_scatter(shard, axes[0], scatter_dimension=dim, tiled=True)  52.9 us
    dot_general x1, matrix products, per_device(): preact = jnp.dot(normed, weight, preferred_element_type=jnp.float32)  14.8 us
    dot_general x1, matrix products, per_device(): lax.dot_general(pre_grad, weight, (((1,), (1,)), ((), ())), preferred_ele...  14.6 us
    dot_general x1, matrix products, per_device(): lax.dot_general(normed, pre_grad, (((0,), (0,)), ((), ())), preferred_ele...  14.2 us
    all_to_all x1, blocking collectives, copy_for_each(): lax.all_to_all(jnp.broadcast_to(shard[None], (length, *shard.shape)), axi...  10.3 us
    convert_element_type x1, other arithmetic, per_device(): inputs = tokens.astype(jnp.float32)  6.54 us
  transfers between devices with their start and end apart: 4, of which 4 were waited for; matrix products, arithmetic and copies ran while one was open for 9% of the time, Pallas kernels for 0%

commit v1 on v0

v1 whole, which is shorter than its diff:
```python
import jax
import jax.numpy as jnp
from jax import lax
from jax.experimental import pallas as pl
from jax.experimental.pallas import tpu as pltpu
from jax.sharding import PartitionSpec as P

MESH = pl.DeviceIdType.MESH
F32, BF16 = jnp.float32, jnp.bfloat16

D = 4096
TOK = 512
CW = 1792
HALF = 896
BLK = 128
CH = HALF // BLK
CR = 512
R1 = 224
R2 = CR - R1
H1, H2 = R1 // 2, R2 // 2
NB = 4
TB = TOK // NB
XS = D // 4
WS = D // 8


def hadamard():
    both = lax.broadcasted_iota(jnp.int32, (BLK, BLK), 0) & lax.broadcasted_iota(
        jnp.int32, (BLK, BLK), 1
    )
    for shift in (4, 2, 1):
        both = both ^ lax.shift_right_logical(both, shift)
    return (1 - 2 * (both & 1)).astype(F32).astype(BF16)


class Lane:
    def __init__(self, send_sems, recv_sems):
        self.send_sems, self.recv_sems, self.kinds, self.rows = send_sems, recv_sems, {}, {}

    def add(self, name, src, dst, device, land):
        self.rows[name] = len(self.kinds)
        self.kinds[name] = (src, dst, device, land)

    def start(self, name, k):
        src, dst, device, _ = self.kinds[name]
        row = self.rows[name]
        pltpu.make_async_remote_copy(
            src_ref=src(k),
            dst_ref=dst(k),
            send_sem=self.send_sems.at[row, k],
            recv_sem=self.recv_sems.at[row, k],
            device_id=device,
            device_id_type=MESH,
        ).start()

    def arrived(self, name, k):
        _, _, device, land = self.kinds[name]
        row = self.rows[name]
        pltpu.make_async_remote_copy(
            src_ref=land(k),
            dst_ref=land(k),
            send_sem=self.send_sems.at[row, k],
            recv_sem=self.recv_sems.at[row, k],
            device_id=device,
            device_id_type=MESH,
        ).wait_recv()

    def sent(self, name, k):
        src, dst, device, _ = self.kinds[name]
        row = self.rows[name]
        pltpu.make_async_remote_copy(
            src_ref=src(k),
            dst_ref=dst(k),
            send_sem=self.send_sems.at[row, k],
            recv_sem=self.recv_sems.at[row, k],
            device_id=device,
            device_id_type=MESH,
        ).wait_send()

    def drain(self, count):
        @pl.loop(0, count)
        def _(k):
            for name in self.kinds:
                self.sent(name, k)


def kernel(
    tokens, gain, coded, codes, grid, cot,
    act_out, wg_out, ig_out,
    cod, wsib, w, normed, pg, act, g, fin,
    ng, nr, xf, xn, hs, hr, ho, tsl, igv,
    inv, rdacc, rdo, rdr, rdw,
    ry1, rf, rg, rn, rm, ry2,
    loc, act_sem, wg_sem, ig_sem,
    ag_s, ag_r, rs_s, rs_r, sw_s, sw_r, nm_s, nm_r, x_s, x_r, rd_s, rd_r, rw_s, rw_r, ct_s, ct_r,
):
    wi, ni = lax.axis_index("wide"), lax.axis_index("narrow")
    x, yh = wi // 2, wi % 2
    yl, z, c = ni // 8, (ni // 2) % 4, ni % 2
    zp, zm, z2 = (z + 1) % 4, (z + 3) % 4, (z + 2) % 4
    xp, xm, x2 = (x + 1) % 4, (x + 3) % 4, (x + 2) % 4
    yo = 1 - yl
    dev_zp = (wi, (yl * 4 + zp) * 2 + c)
    dev_zm = (wi, (yl * 4 + zm) * 2 + c)
    dev_y = (wi, (yo * 4 + z) * 2 + c)
    dev_c = (wi, (yl * 4 + z) * 2 + (1 - c))
    dev_xp = (xp * 2 + yh, ni)
    dev_xm = (xm * 2 + yh, ni)
    dev_h = (x * 2 + (1 - yh), ni)
    dev_w = [((wi + r) % 8, ni) for r in range(1, 8)]

    def cols(k):
        return pl.ds(pl.multiple_of(k * BLK, BLK), BLK)

    def wide_cols(core, k):
        return pl.ds(pl.multiple_of(core * HALF + k * BLK, BLK), BLK)

    def trows(j, base=0):
        return pl.ds(pl.multiple_of(base + j * TB, TB), TB)

    mine = pl.ds(pl.multiple_of(c * 256, 256), 256)
    other = pl.ds(pl.multiple_of((1 - c) * 256, 256), 256)

    load_cod = pltpu.make_async_copy(coded, cod, loc.at[0])
    load_tok = pltpu.make_async_copy(tokens, ng.at[pl.ds(0, TOK)], loc.at[1])
    load_cot = pltpu.make_async_copy(
        cot.at[:, pl.ds(pl.multiple_of(c * HALF, BLK), HALF)], pg.at[pl.ds(0, TOK)], loc.at[2]
    )
    load_tsl = pltpu.make_async_copy(
        tokens.at[:, pl.ds(pl.multiple_of(wi * WS, BLK), WS)], tsl, loc.at[3]
    )
    load_cod.start()
    load_tok.start()
    load_cot.start()
    load_tsl.start()

    barrier = pltpu.get_barrier_semaphore()
    partners = [dev_zp, dev_zm, dev_y, dev_c, *dev_w]
    for device in partners:
        pl.semaphore_signal(barrier, inc=1, device_id=device, device_id_type=MESH)
    pl.semaphore_wait(barrier, len(partners))

    swap = Lane(sw_s, sw_r)
    swap.add(
        "w",
        lambda k: wsib.at[:, cols(k)],
        lambda k: w.at[yl, z, mine, cols(k)],
        dev_c,
        lambda k: w.at[yl, z, other, cols(k)],
    )
    cts = Lane(ct_s, ct_r)
    cts.add(
        "c",
        lambda k: cot.at[:, pl.ds(pl.multiple_of((1 - c) * HALF, BLK), HALF)],
        lambda k: pg.at[pl.ds(TOK, TOK)],
        dev_c,
        lambda k: pg.at[pl.ds(TOK, TOK)],
    )
    nms = Lane(nm_s, nm_r)
    nms.add(
        "n",
        lambda j: normed.at[trows(j)],
        lambda j: normed.at[trows(j, TOK)],
        dev_c,
        lambda j: normed.at[trows(j, TOK)],
    )

    ag = Lane(ag_s, ag_r)

    def piece(name, device, src_at, land_at, lo, n):
        ag.add(
            name,
            lambda k: w.at[src_at[0], src_at[1], pl.ds(lo, n), cols(k)],
            lambda k: w.at[src_at[0], src_at[1], pl.ds(lo, n), cols(k)],
            device,
            lambda k: w.at[land_at[0], land_at[1], pl.ds(lo, n), cols(k)],
        )

    piece("own_zp", dev_zp, (yl, z), (yl, zm), 0, CR)
    piece("own_zm", dev_zm, (yl, z), (yl, zp), 0, CR)
    piece("own_y", dev_y, (yl, z), (yo, z), 0, CR)
    piece("far_zp", dev_zp, (yl, zm), (yl, z2), 0, CR // 2)
    piece("far_zm", dev_zm, (yl, zp), (yl, z2), CR // 2, CR // 2)
    piece("zm_y", dev_y, (yl, zm), (yo, zm), 0, R1)
    piece("zp_y", dev_y, (yl, zp), (yo, zp), 0, R1)
    piece("y_zp", dev_zp, (yo, z), (yo, zm), R1, R2)
    piece("y_zm", dev_zm, (yo, z), (yo, zp), R1, R2)
    piece("z2_y", dev_y, (yl, z2), (yo, z2), 0, R1)
    piece("yfar_zp", dev_zp, (yo, zm), (yo, z2), R1, H2)
    piece("yfar_zm", dev_zm, (yo, zp), (yo, z2), R1 + H2, H2)

    def ag_a(k):
        swap.arrived("w", k)
        ag.start("own_zp", k)
        ag.start("own_zm", k)
        ag.start("own_y", k)

    def ag_b(k):
        ag.arrived("own_y", k)
        ag.start("y_zp", k)
        ag.start("y_zm", k)
        ag.arrived("own_zp", k)
        ag.start("far_zp", k)
        ag.start("zm_y", k)
        ag.arrived("own_zm", k)
        ag.start("far_zm", k)
        ag.start("zp_y", k)

    def ag_c(k):
        ag.arrived("far_zp", k)
        ag.start("z2_y", k)
        ag.arrived("y_zp", k)
        ag.start("yfar_zp", k)
        ag.arrived("y_zm", k)
        ag.start("yfar_zm", k)

    def ag_d(k):
        for name in ("far_zm", "zm_y", "zp_y", "z2_y", "yfar_zp", "yfar_zm"):
            ag.arrived(name, k)

    rs = Lane(rs_s, rs_r)
    rs.add("a_y", lambda k: g.at[yo, :, pl.ds(0, R1), cols(k)], lambda k: ry1.at[k], dev_y,
           lambda k: ry1.at[k])
    rs.add("a_zp", lambda k: g.at[:, z2, pl.ds(R1, H2), cols(k)], lambda k: rf.at[0, k], dev_zp,
           lambda k: rf.at[0, k])
    rs.add("a_zm", lambda k: g.at[:, z2, pl.ds(R1 + H2, H2), cols(k)], lambda k: rf.at[1, k],
           dev_zm, lambda k: rf.at[1, k])
    rs.add("b1_zp", lambda k: g.at[yl, z2, pl.ds(0, H1), cols(k)], lambda k: rg.at[0, k], dev_zp,
           lambda k: rg.at[0, k])
    rs.add("b1_zm", lambda k: g.at[yl, z2, pl.ds(H1, H1), cols(k)], lambda k: rg.at[1, k], dev_zm,
           lambda k: rg.at[1, k])
    rs.add("b2_zp", lambda k: g.at[:, zp, pl.ds(R1, R2), cols(k)], lambda k: rn.at[0, k], dev_zp,
           lambda k: rn.at[0, k])
    rs.add("b2_zm", lambda k: g.at[:, zm, pl.ds(R1, R2), cols(k)], lambda k: rn.at[1, k], dev_zm,
           lambda k: rn.at[1, k])
    rs.add("c_zp", lambda k: g.at[yl, zp, pl.ds(0, R1), cols(k)], lambda k: rm.at[0, k], dev_zp,
           lambda k: rm.at[0, k])
    rs.add("c_zm", lambda k: g.at[yl, zm, pl.ds(0, R1), cols(k)], lambda k: rm.at[1, k], dev_zm,
           lambda k: rm.at[1, k])
    rs.add("c_y", lambda k: g.at[yo, z, pl.ds(R1, R2), cols(k)], lambda k: ry2.at[k], dev_y,
           lambda k: ry2.at[k])

    def plus(first, *rest):
        total = first.astype(F32)
        for term in rest:
            total = total + term.astype(F32)
        return total

    def add_into(at, *terms):
        g[at] = plus(g[at], *terms).astype(BF16)

    def rs_a(k):
        rs.start("a_y", k)
        rs.start("a_zp", k)
        rs.start("a_zm", k)

    def rs_b(k):
        rs.arrived("a_zp", k)
        add_into((slice(None), zp, pl.ds(R1, H2), cols(k)), rf[0, k])
        rs.start("b2_zp", k)
        rs.arrived("a_zm", k)
        add_into((slice(None), zm, pl.ds(R1 + H2, H2), cols(k)), rf[1, k])
        rs.start("b2_zm", k)
        rs.arrived("a_y", k)
        add_into((yl, slice(None), pl.ds(0, R1), cols(k)), ry1[k])
        rs.start("b1_zp", k)
        rs.start("b1_zm", k)

    def rs_c(k):
        rs.arrived("b2_zp", k)
        rs.arrived("b2_zm", k)
        add_into((slice(None), z, pl.ds(R1, R2), cols(k)), rn[0, k], rn[1, k])
        rs.start("c_y", k)
        rs.arrived("b1_zp", k)
        add_into((yl, zp, pl.ds(0, H1), cols(k)), rg[0, k])
        rs.start("c_zp", k)
        rs.arrived("b1_zm", k)
        add_into((yl, zm, pl.ds(H1, H1), cols(k)), rg[1, k])
        rs.start("c_zm", k)

    def wg_local(k):
        return pltpu.make_async_copy(
            fin.at[mine, cols(k)], wg_out.at[:, wide_cols(c, k)], wg_sem.at[0, k]
        )

    def wg_remote(k, landed=False):
        target = wg_out.at[:, wide_cols((1 - c) if landed else c, k)]
        return pltpu.make_async_remote_copy(
            src_ref=fin.at[other, cols(k)],
            dst_ref=target,
            send_sem=wg_sem.at[1, k],
            recv_sem=wg_sem.at[2, k],
            device_id=dev_c,
            device_id_type=MESH,
        )

    def rs_d(k):
        rs.arrived("c_zp", k)
        rs.arrived("c_zm", k)
        fin[pl.ds(0, R1), cols(k)] = plus(g[yl, z, pl.ds(0, R1), cols(k)], rm[0, k], rm[1, k])
        rs.arrived("c_y", k)
        fin[pl.ds(R1, R2), cols(k)] = plus(g[yl, z, pl.ds(R1, R2), cols(k)], ry2[k])
        wg_local(k).start()
        wg_remote(k).start()

    def act_local(k):
        return pltpu.make_async_copy(
            act.at[pl.ds(0, TOK), cols(k)], act_out.at[:, wide_cols(c, k)], act_sem.at[0, k]
        )

    def act_remote(k, landed=False):
        return pltpu.make_async_remote_copy(
            src_ref=act.at[pl.ds(TOK, TOK), cols(k)],
            dst_ref=act_out.at[:, wide_cols((1 - c) if landed else c, k)],
            send_sem=act_sem.at[1, k],
            recv_sem=act_sem.at[2, k],
            device_id=dev_c,
            device_id_type=MESH,
        )

    def compute(k):
        @pl.loop(0, 4)
        def _(t):
            rows = pl.ds(pl.multiple_of(t * 256, 256), 256)
            weight = w[:, :, :, cols(k)].reshape(D, BLK)
            preact = jnp.dot(normed[rows], weight, preferred_element_type=F32)
            sig = 1.0 / (1.0 + jnp.exp(-preact))
            act[rows, cols(k)] = (preact * sig).astype(BF16)
            grad = (pg[rows, cols(k)].astype(F32) * sig * (1.0 + preact * (1.0 - sig))).astype(BF16)
            pg[rows, cols(k)] = grad
            rdacc[rows] += preact * grad.astype(F32)

        act_local(k).start()
        act_remote(k).start()
        turned = pg[:, cols(k)].T
        for q in range(8):
            part = jnp.dot(turned, normed[:, q * CR : (q + 1) * CR], preferred_element_type=F32)
            g[q // 4, q % 4, :, cols(k)] = part.T.astype(BF16)

    xs = Lane(x_s, x_r)

    def span(start, n):
        return pl.ds(pl.multiple_of(start, BLK), n)

    xs.add("sib", lambda j: ng.at[trows(j, TOK)], lambda j: nr.at[trows(j)], dev_c,
           lambda j: nr.at[trows(j)])
    xs.add("far_p", lambda j: ng.at[trows(j), span(x2 * XS, WS)], lambda j: xf.at[0, trows(j)],
           dev_xp, lambda j: xf.at[0, trows(j)])
    xs.add("far_m", lambda j: ng.at[trows(j), span(x2 * XS + WS, WS)], lambda j: xf.at[1, trows(j)],
           dev_xm, lambda j: xf.at[1, trows(j)])
    xs.add("near_p", lambda j: ng.at[trows(j), span(xp * XS, XS)], lambda j: xn.at[0, trows(j)],
           dev_xp, lambda j: xn.at[0, trows(j)])
    xs.add("near_m", lambda j: ng.at[trows(j), span(xm * XS, XS)], lambda j: xn.at[1, trows(j)],
           dev_xm, lambda j: xn.at[1, trows(j)])
    xs.add("h", lambda j: hs.at[trows(j)], lambda j: hr.at[trows(j)], dev_h,
           lambda j: hr.at[trows(j)])

    def ng_p(j):
        grads = jnp.concatenate([pg[trows(j)], pg[trows(j, TOK)]], axis=0)
        for q in range(8):
            part = lax.dot_general(
                grads, w[q // 4, q % 4], (((1,), (1,)), ((), ())), preferred_element_type=F32
            ).astype(BF16)
            ng[trows(j), q * CR : (q + 1) * CR] = part[:TB]
            ng[trows(j, TOK), q * CR : (q + 1) * CR] = part[TB:]
        xs.start("sib", j)

    def ng_q(j):
        xs.arrived("sib", j)
        ng[trows(j)] = plus(ng[trows(j)], nr[trows(j)]).astype(BF16)
        xs.start("far_p", j)
        xs.start("far_m", j)

    def ng_r(j):
        xs.arrived("far_p", j)
        at = (trows(j), span(xp * XS, WS))
        ng[at] = plus(ng[at], xf[0, trows(j)]).astype(BF16)
        xs.start("near_p", j)
        xs.arrived("far_m", j)
        at = (trows(j), span(xm * XS + WS, WS))
        ng[at] = plus(ng[at], xf[1, trows(j)]).astype(BF16)
        xs.start("near_m", j)

    def ng_u(j):
        xs.arrived("near_p", j)
        xs.arrived("near_m", j)
        theirs, ours = span((1 - yh) * WS, WS), span(yh * WS, WS)
        base = x * XS
        hs[trows(j)] = plus(
            ng[trows(j), span(base + (1 - yh) * WS, WS)],
            xn[0, trows(j), theirs],
            xn[1, trows(j), theirs],
        ).astype(BF16)
        xs.start("h", j)
        ho[trows(j)] = plus(
            ng[trows(j), span(base + yh * WS, WS)], xn[0, trows(j), ours], xn[1, trows(j), ours]
        )

    def ig_copy(j):
        return pltpu.make_async_copy(igv.at[trows(j)], ig_out.at[trows(j)], ig_sem.at[j])

    def ng_v(j):
        xs.arrived("h", j)
        scaled = plus(ho[trows(j)], hr[trows(j)]) * gain[:, span(wi * WS, WS)]
        scale = inv[trows(j)][:, :1]
        dots = rdacc[trows(j)][:, :1]
        igv[trows(j)] = (scale * scaled - tsl[trows(j)].astype(F32) * (scale * scale) * dots).astype(
            BF16
        )
        ig_copy(j).start()

    rds = Lane(rd_s, rd_r)
    rds.add("s", lambda k: rdo.at[1], lambda k: rdr, dev_c, lambda k: rdr)
    rws = Lane(rw_s, rw_r)
    for r in range(7):
        rws.add(str(r), lambda k: rdo.at[0], lambda k, r=r: rdw.at[r], dev_w[r],
                lambda k, r=r: rdw.at[r])

    def rd_1():
        ones = jnp.ones((8, BLK), F32)
        for half in range(2):
            rdo[half] = lax.dot_general(
                ones,
                rdacc[half * TOK : (half + 1) * TOK],
                (((1,), (1,)), ((), ())),
                precision=lax.Precision.HIGHEST,
                preferred_element_type=F32,
            )
        rds.start("s", 0)

    def rd_2():
        rds.arrived("s", 0)
        rdo[0] = rdo[0] + rdr[...]
        for r in range(7):
            rws.start(str(r), 0)

    def rd_3():
        for r in range(7):
            rws.arrived(str(r), 0)
        total = rdo[0]
        for r in range(7):
            total = total + rdw[r]
        rdacc[pl.ds(0, TOK)] = jnp.broadcast_to((total / D).T[:, :1], (TOK, BLK))

    cts.start("c", 0)
    rotation = hadamard()
    load_cod.wait()

    def decoded(core, k):
        at = wide_cols(core, k)
        turned = jnp.dot(cod[:, at], rotation, preferred_element_type=F32)
        block = core * CH + k
        norm = 1.0 / (BLK**0.5)
        top = turned[:BLK] * (grid[codes[0, block]] * norm)
        low = turned[BLK:] * (grid[codes[1, block]] * norm)
        return jnp.concatenate([top, low], axis=0).astype(BF16)

    @pl.loop(0, CH)
    def _(k):
        wsib[:, cols(k)] = decoded(1 - c, k)
        swap.start("w", k)
        w[yl, z, mine, cols(k)] = decoded(c, k)

    ag_a(0)
    ag_a(1)
    rdacc[...] = jnp.zeros_like(rdacc)
    load_tok.wait()

    @pl.loop(0, NB)
    def _(j):
        @pl.loop(0, TB // 32)
        def _(i):
            rows = pl.ds(pl.multiple_of(j * TB + i * 32, 32), 32)
            values = ng[rows].astype(F32)
            scale = lax.rsqrt(jnp.sum(values * values, axis=-1, keepdims=True) * (1.0 / D) + 1e-5)
            inv[rows] = jnp.broadcast_to(scale, (32, BLK))
            normed[rows] = (values * scale * gain[...]).astype(BF16)

        nms.start("n", j)

    @pl.loop(0, CH + 2)
    def _(s):
        @pl.when(s + 2 < CH)
        def _():
            ag_a(s + 2)

        @pl.when(s < CH)
        def _():
            ag_b(s)

        @pl.when((s >= 1) & (s < CH + 1))
        def _():
            ag_c(s - 1)

        @pl.when(s >= CH)
        def _():
            rs_a(s - CH)

        @pl.when(s == 2)
        def _():
            load_cot.wait()
            cts.arrived("c", 0)
            for j in range(NB):
                nms.arrived("n", j)

        @pl.when(s >= 2)
        def _():
            ag_d(s - 2)
            compute(s - 2)

    rd_1()

    @pl.loop(0, CH + 2)
    def _(t):
        @pl.when(t + 2 < CH)
        def _():
            rs_a(t + 2)

        @pl.when(t < NB)
        def _():
            ng_p(t)

        @pl.when(t < CH)
        def _():
            rs_b(t)

        @pl.when(t < NB)
        def _():
            ng_q(t)

        @pl.when((t >= 1) & (t < CH + 1))
        def _():
            rs_c(t - 1)

        @pl.when(t == 1)
        def _():
            rd_2()

        @pl.when((t >= 2) & (t < NB + 2))
        def _():
            ng_r(t - 2)

        @pl.when(t >= 2)
        def _():
            rs_d(t - 2)

        @pl.when(t == 3)
        def _():
            load_tsl.wait()
            rd_3()

        @pl.when((t >= 4) & (t < NB + 4))
        def _():
            ng_u(t - 4)

        @pl.when((t >= 5) & (t < NB + 5))
        def _():
            ng_v(t - 5)

    swap.drain(CH)
    ag.drain(CH)
    rs.drain(CH)
    nms.drain(NB)
    xs.drain(NB)
    cts.sent("c", 0)
    rds.sent("s", 0)
    for r in range(7):
        rws.sent(str(r), 0)

    @pl.loop(0, CH)
    def _(k):
        act_local(k).wait()
        act_remote(k).wait_send()
        act_remote(k, True).wait_recv()
        wg_local(k).wait()
        wg_remote(k).wait_send()
        wg_remote(k, True).wait_recv()

    @pl.loop(0, NB)
    def _(j):
        ig_copy(j).wait()


def per_device(tokens, norm_gain, coded, block_codes, grid, cotangent):
    anywhere = pl.BlockSpec(memory_space=pl.ANY)
    vmem = pl.BlockSpec(memory_space=pltpu.VMEM)
    smem = pl.BlockSpec(memory_space=pltpu.SMEM)
    sem = pltpu.SemaphoreType.DMA
    return pl.pallas_call(
        kernel,
        out_shape=(
            jax.ShapeDtypeStruct((TOK, CW), BF16),
            jax.ShapeDtypeStruct((D // 16, CW), F32),
            jax.ShapeDtypeStruct((TOK, WS), BF16),
        ),
        in_specs=[anywhere, vmem, anywhere, smem, smem, anywhere],
        out_specs=(anywhere, anywhere, anywhere),
        scratch_shapes=[
            pltpu.VMEM((256, CW), BF16),
            pltpu.VMEM((256, HALF), BF16),
            pltpu.VMEM((2, 4, CR, HALF), BF16),
            pltpu.VMEM((2 * TOK, D), BF16),
            pltpu.VMEM((2 * TOK, HALF), BF16),
            pltpu.VMEM((2 * TOK, HALF), BF16),
            pltpu.VMEM((2, 4, CR, HALF), BF16),
            pltpu.VMEM((CR, HALF), F32),
            pltpu.VMEM((2 * TOK, D), BF16),
            pltpu.VMEM((TOK, D), BF16),
            pltpu.VMEM((2, TOK, WS), BF16),
            pltpu.VMEM((2, TOK, XS), BF16),
            pltpu.VMEM((TOK, WS), BF16),
            pltpu.VMEM((TOK, WS), BF16),
            pltpu.VMEM((TOK, WS), F32),
            pltpu.VMEM((TOK, WS), BF16),
            pltpu.VMEM((TOK, WS), BF16),
            pltpu.VMEM((TOK, BLK), F32),
            pltpu.VMEM((2 * TOK, BLK), F32),
            pltpu.VMEM((2, 8, TOK), F32),
            pltpu.VMEM((8, TOK), F32),
            pltpu.VMEM((7, 8, TOK), F32),
            pltpu.VMEM((CH, 4, R1, BLK), BF16),
            pltpu.VMEM((2, CH, 2, H2, BLK), BF16),
            pltpu.VMEM((2, CH, H1, BLK), BF16),
            pltpu.VMEM((2, CH, 2, R2, BLK), BF16),
            pltpu.VMEM((2, CH, R1, BLK), BF16),
            pltpu.VMEM((CH, R2, BLK), BF16),
            sem((4,)), sem((3, CH)), sem((3, CH)), sem((NB,)),
            sem((12, CH)), sem((12, CH)), sem((10, CH)), sem((10, CH)),
            sem((1, CH)), sem((1, CH)), sem((1, NB)), sem((1, NB)),
            sem((6, NB)), sem((6, NB)), sem((1, 1)), sem((1, 1)),
            sem((7, 1)), sem((7, 1)), sem((1, 1)), sem((1, 1)),
        ],
        compiler_params=pltpu.CompilerParams(
            collective_id=0, has_side_effects=True, vmem_limit_bytes=63 << 20
        ),
        cost_estimate=pl.CostEstimate(
            flops=6 * TOK * D * CW, bytes_accessed=40 << 20, transcendentals=TOK * CW
        ),
    )(tokens, norm_gain.reshape(1, D), coded, block_codes, grid, cotangent)


def solution(mesh):
    placed = (
        P("narrow", None), P(), P("narrow", "wide"), P("narrow", "wide"), P(), P("narrow", "wide"),
    )
    return jax.shard_map(
        per_device,
        mesh=mesh,
        in_specs=placed,
        out_specs=(P("narrow", "wide"), P("narrow", "wide"), P("narrow", "wide")),
        check_vma=False,
    )
```

time: 301 us -> 132 us (0.44)
  waiting for transfers between devices: 209 us -> 0 us
  Pallas kernels: 0 us -> 126 us
  matrix products: 44.4 us -> 0 us
  other arithmetic: 16.4 us -> 0 us
  between operations: 13.9 us -> 0.65 us
  blocking collectives: 10.3 us -> 0 us
    reduce_scatter x3 -> x0, waiting for transfers between devices: 126 us -> none  [the longest x1 73.5 us: per_device(): lax.psum_scatter(lax.dot_general(normed, pre_grad, (((0,), (0,)), ((), ()...]
    pallas_call x0 -> x1, Pallas kernels: none -> 126 us  [per_device(): pl.pallas_call(kernel, out_shape=(jax.ShapeDtypeStruct((TOK, CW), BF16),...]
    all_gather x1 -> x0, waiting for transfers between devices: 82.4 us -> none  [per_device(): lax.all_gather(decode(coded, block_codes, grid), 'narrow', axis=0, tiled=...]
    dot_general x5 -> x0, matrix products: 44.4 us -> none  [the longest x1 14.8 us: per_device(): preact = jnp.dot(normed, weight, preferred_element_type=jnp.float32)]
    convert_element_type x3 -> x0, other arithmetic: 11.5 us -> none  [the longest x1 6.54 us: per_device(): inputs = tokens.astype(jnp.float32)]
    all_to_all x1 -> x0, blocking collectives: 10.3 us -> none  [copy_for_each(): lax.all_to_all(jnp.broadcast_to(shard[None], (length, *shard.shape)), axi...]
    reduce_sum x4 -> x0, other arithmetic: 4.87 us -> none  [the longest x1 3.08 us: per_device(): jnp.mean(inputs * inputs, axis=-1, keepdims=True) + 1e-05]
  transfers between devices with their start and end apart: 4 -> 0, of which waited for: 4 -> 0; matrix products, arithmetic and copies ran while one was open for 9% -> 0% of each run, Pallas kernels for 0% -> 0%
where the time goes in v1:
time: 132 us
  Pallas kernels  126 us (95%)
  local copies, waits for them, and re-layouts  5.17 us (4%)
    pallas_call x1, Pallas kernels, per_device(): pl.pallas_call(kernel, out_shape=(jax.ShapeDtypeStruct((TOK, CW), BF16),...  126 us
    unnamed x7, local copies, waits for them, and re-layouts  5.17 us

profile of v1, /device:TPU:1, one launch (start us, length us, event | category | flops | bytes accessed | tf_op | source)
XLA Modules:
  0.0 131.8 jit_solution(13725670784701594976)
XLA Ops:
  0.6 125.9 %shard_map.85 = (bf16[512,1792]{1,0:T(8,128)(2,1)}, f32[256,1792]{1,0:T(8,128)}, bf16[512,512]{1,0:T(8,128)(2,1)}) custom-call(bf16[512,4096]{1,0:T(8,128)(2,1)} %tokens.1, f32[1,4096]{1,0:T(1,128)} %bitcast.1, bf16[256,1792]{1,0:T(8,128)(2,1)} %coded.1, s32[2,14]{1,0:T(2,128)} %codes.1, f32[16]{0:T(128)} %grid.1, bf16[512,1792]{1,0:T(8,128)(2,1)} %cot.1), custom_call_target="tpu_custom_call" | custom-call | flops 22548578304 | bytes 41943040 | tf_op jit(solution)/shard_map/pallas_call | solution.py:589
  126.6 0.0 copy-start
  126.6 3.0 %copy.12 = bf16[512,1792]{1,0:T(8,128)(2,1)} copy(bf16[512,1792]{1,0:T(8,128)(2,1)} %get-tuple-element.6) | data formatting | bytes 3670016
  129.6 0.0 copy-done
  129.6 0.0 copy-start.1
  129.6 1.2 copy.13
  130.8 0.2 copy-done.1
  131.0 0.8 copy.14
Async XLA Ops:
  126.6 3.0 %copy-start = (f32[256,1792]{1,0:T(8,128)S(1)}, f32[256,1792]{1,0:T(8,128)}, u32[]{:S(2)}) copy-start(f32[256,1792]{1,0:T(8,128)} %get-tuple-element.7) | copy-start | bytes 5505028
  129.6 1.4 %copy-start.1 = (bf16[512,512]{1,0:T(8,128)(2,1)S(1)}, bf16[512,512]{1,0:T(8,128)(2,1)}, u32[]{:S(2)}) copy-start(bf16[512,512]{1,0:T(8,128)(2,1)} %get-tuple-element.8) | copy-start | bytes 1572868

commit v2 on v1

--- a/solution.py
+++ b/solution.py
@@ -15,14 +15,23 @@
 BLK = 128
 CH = HALF // BLK
 CR = 512
-R1 = 224
+G1 = 224
+G2, GH = CR - G1, (CR - G1) // 2
+R1 = 160
 R2 = CR - R1
 H1, H2 = R1 // 2, R2 // 2
-NB = 4
+KP = 4 * BLK
+NB = 8
 TB = TOK // NB
 XS = D // 4
 WS = D // 8
 
+LA, LC, LD = 1, 1, 2
+RC, RD = 1, 3
+NR, NU, NV = 2, 4, 5
+ER, EU = 2, 2
+STEPS = CH - 1 + LD + max(CH + RD, NV + NB // EU)
+
 
 def hadamard():
     both = lax.broadcasted_iota(jnp.int32, (BLK, BLK), 0) & lax.broadcasted_iota(
@@ -37,51 +46,32 @@
     def __init__(self, send_sems, recv_sems):
         self.send_sems, self.recv_sems, self.kinds, self.rows = send_sems, recv_sems, {}, {}
 
-    def add(self, name, src, dst, device, land):
+    def add(self, name, src, dst, device, land, whole):
         self.rows[name] = len(self.kinds)
-        self.kinds[name] = (src, dst, device, land)
+        self.kinds[name] = (src, dst, device, land, whole)
+
+    def copy(self, name, k, src, dst):
+        row = self.rows[name]
+        return pltpu.make_async_remote_copy(
+            src_ref=src,
+            dst_ref=dst,
+            send_sem=self.send_sems.at[row],
+            recv_sem=self.recv_sems.at[row, k],
+            device_id=self.kinds[name][2],
+            device_id_type=MESH,
+        )
 
     def start(self, name, k):
-        src, dst, device, _ = self.kinds[name]
-        row = self.rows[name]
-        pltpu.make_async_remote_copy(
-            src_ref=src(k),
-            dst_ref=dst(k),
-            send_sem=self.send_sems.at[row, k],
-            recv_sem=self.recv_sems.at[row, k],
-            device_id=device,
-            device_id_type=MESH,
-        ).start()
+        src, dst, _, _, _ = self.kinds[name]
+        self.copy(name, k, src(k), dst(k)).start()
 
     def arrived(self, name, k):
-        _, _, device, land = self.kinds[name]
-        row = self.rows[name]
-        pltpu.make_async_remote_copy(
-            src_ref=land(k),
-            dst_ref=land(k),
-            send_sem=self.send_sems.at[row, k],
-            recv_sem=self.recv_sems.at[row, k],
-            device_id=device,
-            device_id_type=MESH,
-        ).wait_recv()
-
-    def sent(self, name, k):
-        src, dst, device, _ = self.kinds[name]
-        row = self.rows[name]
-        pltpu.make_async_remote_copy(
-            src_ref=src(k),
-            dst_ref=dst(k),
-            send_sem=self.send_sems.at[row, k],
-            recv_sem=self.recv_sems.at[row, k],
-            device_id=device,
-            device_id_type=MESH,
-        ).wait_send()
-
-    def drain(self, count):
-        @pl.loop(0, count)
-        def _(k):
-            for name in self.kinds:
-                self.sent(name, k)
+        land = self.kinds[name][3]
+        self.copy(name, k, land(k), land(k)).wait_recv()
+
+    def drain(self):
+        for name, (_, _, _, _, whole) in self.kinds.items():
+            self.copy(name, 0, whole, whole).wait_send()
 
 
 def kernel(
@@ -92,7 +82,7 @@
     inv, rdacc, rdo, rdr, rdw,
     ry1, rf, rg, rn, rm, ry2,
     loc, act_sem, wg_sem, ig_sem,
-    ag_s, ag_r, rs_s, rs_r, sw_s, sw_r, nm_s, nm_r, x_s, x_r, rd_s, rd_r, rw_s, rw_r, ct_s, ct_r,
+    ag_s, ag_r, rs_s, rs_r, si_s, si_r, sw_s, sw_r, nm_s, nm_r, x_s, x_r, rd_s, rd_r, rw_s, rw_r, ct_s, ct_r,
 ):
     wi, ni = lax.axis_index("wide"), lax.axis_index("narrow")
     x, yh = wi // 2, wi % 2
@@ -130,14 +120,14 @@
         tokens.at[:, pl.ds(pl.multiple_of(wi * WS, BLK), WS)], tsl, loc.at[3]
     )
     load_cod.start()
-    load_tok.start()
-    load_cot.start()
-    load_tsl.start()
-
     barrier = pltpu.get_barrier_semaphore()
     partners = [dev_zp, dev_zm, dev_y, dev_c, *dev_w]
     for device in partners:
         pl.semaphore_signal(barrier, inc=1, device_id=device, device_id_type=MESH)
+    load_tok.start()
+    load_cot.start()
+    load_tsl.start()
+    load_cod.wait()
     pl.semaphore_wait(barrier, len(partners))
 
     swap = Lane(sw_s, sw_r)
@@ -147,6 +137,7 @@
         lambda k: w.at[yl, z, mine, cols(k)],
         dev_c,
         lambda k: w.at[yl, z, other, cols(k)],
+        wsib,
     )
     cts = Lane(ct_s, ct_r)
     cts.add(
@@ -155,6 +146,7 @@
         lambda k: pg.at[pl.ds(TOK, TOK)],
         dev_c,
         lambda k: pg.at[pl.ds(TOK, TOK)],
+        pg.at[pl.ds(TOK, TOK)],
     )
     nms = Lane(nm_s, nm_r)
     nms.add(
@@ -163,6 +155,7 @@
         lambda j: normed.at[trows(j, TOK)],
         dev_c,
         lambda j: normed.at[trows(j, TOK)],
+        normed.at[pl.ds(TOK, TOK)],
     )
 
     ag = Lane(ag_s, ag_r)
@@ -174,6 +167,7 @@
             lambda k: w.at[src_at[0], src_at[1], pl.ds(lo, n), cols(k)],
             device,
             lambda k: w.at[land_at[0], land_at[1], pl.ds(lo, n), cols(k)],
+            w.at[src_at[0], src_at[1], pl.ds(lo, n)],
         )
 
     piece("own_zp", dev_zp, (yl, z), (yl, zm), 0, CR)
@@ -181,13 +175,13 @@
     piece("own_y", dev_y, (yl, z), (yo, z), 0, CR)
     piece("far_zp", dev_zp, (yl, zm), (yl, z2), 0, CR // 2)
     piece("far_zm", dev_zm, (yl, zp), (yl, z2), CR // 2, CR // 2)
-    piece("zm_y", dev_y, (yl, zm), (yo, zm), 0, R1)
-    piece("zp_y", dev_y, (yl, zp), (yo, zp), 0, R1)
-    piece("y_zp", dev_zp, (yo, z), (yo, zm), R1, R2)
-    piece("y_zm", dev_zm, (yo, z), (yo, zp), R1, R2)
-    piece("z2_y", dev_y, (yl, z2), (yo, z2), 0, R1)
-    piece("yfar_zp", dev_zp, (yo, zm), (yo, z2), R1, H2)
-    piece("yfar_zm", dev_zm, (yo, zp), (yo, z2), R1 + H2, H2)
+    piece("zm_y", dev_y, (yl, zm), (yo, zm), 0, G1)
+    piece("zp_y", dev_y, (yl, zp), (yo, zp), 0, G1)
+    piece("y_zp", dev_zp, (yo, z), (yo, zm), G1, G2)
+    piece("y_zm", dev_zm, (yo, z), (yo, zp), G1, G2)
+    piece("z2_y", dev_y, (yl, z2), (yo, z2), 0, G1)
+    piece("yfar_zp", dev_zp, (yo, zm), (yo, z2), G1, GH)
+    piece("yfar_zm", dev_zm, (yo, zp), (yo, z2), G1 + GH, GH)
 
     def ag_a(k):
         swap.arrived("w", k)
@@ -220,25 +214,25 @@
 
     rs = Lane(rs_s, rs_r)
     rs.add("a_y", lambda k: g.at[yo, :, pl.ds(0, R1), cols(k)], lambda k: ry1.at[k], dev_y,
-           lambda k: ry1.at[k])
+           lambda k: ry1.at[k], g.at[yo, :, pl.ds(0, R1)])
     rs.add("a_zp", lambda k: g.at[:, z2, pl.ds(R1, H2), cols(k)], lambda k: rf.at[0, k], dev_zp,
-           lambda k: rf.at[0, k])
+           lambda k: rf.at[0, k], g.at[:, z2, pl.ds(R1, H2)])
     rs.add("a_zm", lambda k: g.at[:, z2, pl.ds(R1 + H2, H2), cols(k)], lambda k: rf.at[1, k],
-           dev_zm, lambda k: rf.at[1, k])
+           dev_zm, lambda k: rf.at[1, k], g.at[:, z2, pl.ds(R1 + H2, H2)])
     rs.add("b1_zp", lambda k: g.at[yl, z2, pl.ds(0, H1), cols(k)], lambda k: rg.at[0, k], dev_zp,
-           lambda k: rg.at[0, k])
+           lambda k: rg.at[0, k], g.at[yl, z2, pl.ds(0, H1)])
     rs.add("b1_zm", lambda k: g.at[yl, z2, pl.ds(H1, H1), cols(k)], lambda k: rg.at[1, k], dev_zm,
-           lambda k: rg.at[1, k])
+           lambda k: rg.at[1, k], g.at[yl, z2, pl.ds(H1, H1)])
     rs.add("b2_zp", lambda k: g.at[:, zp, pl.ds(R1, R2), cols(k)], lambda k: rn.at[0, k], dev_zp,
-           lambda k: rn.at[0, k])
+           lambda k: rn.at[0, k], g.at[:, zp, pl.ds(R1, R2)])
     rs.add("b2_zm", lambda k: g.at[:, zm, pl.ds(R1, R2), cols(k)], lambda k: rn.at[1, k], dev_zm,
-           lambda k: rn.at[1, k])
+           lambda k: rn.at[1, k], g.at[:, zm, pl.ds(R1, R2)])
     rs.add("c_zp", lambda k: g.at[yl, zp, pl.ds(0, R1), cols(k)], lambda k: rm.at[0, k], dev_zp,
-           lambda k: rm.at[0, k])
+           lambda k: rm.at[0, k], g.at[yl, zp, pl.ds(0, R1)])
     rs.add("c_zm", lambda k: g.at[yl, zm, pl.ds(0, R1), cols(k)], lambda k: rm.at[1, k], dev_zm,
-           lambda k: rm.at[1, k])
+           lambda k: rm.at[1, k], g.at[yl, zm, pl.ds(0, R1)])
     rs.add("c_y", lambda k: g.at[yo, z, pl.ds(R1, R2), cols(k)], lambda k: ry2.at[k], dev_y,
-           lambda k: ry2.at[k])
+           lambda k: ry2.at[k], g.at[yo, z, pl.ds(R1, R2)])
 
     def plus(first, *rest):
         total = first.astype(F32)
@@ -247,7 +241,10 @@
         return total
 
     def add_into(at, *terms):
-        g[at] = plus(g[at], *terms).astype(BF16)
+        total = g[at]
+        for term in terms:
+            total = total + term
+        g[at] = total
 
     def rs_a(k):
         rs.start("a_y", k)
@@ -318,20 +315,27 @@
             device_id_type=MESH,
         )
 
-    def compute(k):
+    def forward(k, count):
+        at = pl.ds(pl.multiple_of(k * BLK, BLK), count * BLK)
+
         @pl.loop(0, 4)
         def _(t):
             rows = pl.ds(pl.multiple_of(t * 256, 256), 256)
-            weight = w[:, :, :, cols(k)].reshape(D, BLK)
+            weight = w[:, :, :, at].reshape(D, count * BLK)
             preact = jnp.dot(normed[rows], weight, preferred_element_type=F32)
             sig = 1.0 / (1.0 + jnp.exp(-preact))
-            act[rows, cols(k)] = (preact * sig).astype(BF16)
-            grad = (pg[rows, cols(k)].astype(F32) * sig * (1.0 + preact * (1.0 - sig))).astype(BF16)
-            pg[rows, cols(k)] = grad
-            rdacc[rows] += preact * grad.astype(F32)
-
-        act_local(k).start()
-        act_remote(k).start()
+            act[rows, at] = (preact * sig).astype(BF16)
+            grad = (pg[rows, at].astype(F32) * sig * (1.0 + preact * (1.0 - sig))).astype(BF16)
+            pg[rows, at] = grad
+            dots = preact * grad.astype(F32)
+            for i in range(count):
+                rdacc[rows] += dots[:, i * BLK : (i + 1) * BLK]
+
+        for i in range(count):
+            act_local(k + i).start()
+            act_remote(k + i).start()
+
+    def weight_part(k):
         turned = pg[:, cols(k)].T
         for q in range(8):
             part = jnp.dot(turned, normed[:, q * CR : (q + 1) * CR], preferred_element_type=F32)
@@ -342,43 +346,82 @@
     def span(start, n):
         return pl.ds(pl.multiple_of(start, BLK), n)
 
-    xs.add("sib", lambda j: ng.at[trows(j, TOK)], lambda j: nr.at[trows(j)], dev_c,
-           lambda j: nr.at[trows(j)])
     xs.add("far_p", lambda j: ng.at[trows(j), span(x2 * XS, WS)], lambda j: xf.at[0, trows(j)],
-           dev_xp, lambda j: xf.at[0, trows(j)])
+           dev_xp, lambda j: xf.at[0, trows(j)], ng.at[pl.ds(0, TOK), span(0, WS)])
     xs.add("far_m", lambda j: ng.at[trows(j), span(x2 * XS + WS, WS)], lambda j: xf.at[1, trows(j)],
-           dev_xm, lambda j: xf.at[1, trows(j)])
+           dev_xm, lambda j: xf.at[1, trows(j)], ng.at[pl.ds(0, TOK), span(0, WS)])
     xs.add("near_p", lambda j: ng.at[trows(j), span(xp * XS, XS)], lambda j: xn.at[0, trows(j)],
-           dev_xp, lambda j: xn.at[0, trows(j)])
+           dev_xp, lambda j: xn.at[0, trows(j)], ng.at[pl.ds(0, TOK), span(0, XS)])
     xs.add("near_m", lambda j: ng.at[trows(j), span(xm * XS, XS)], lambda j: xn.at[1, trows(j)],
-           dev_xm, lambda j: xn.at[1, trows(j)])
+           dev_xm, lambda j: xn.at[1, trows(j)], ng.at[pl.ds(0, TOK), span(0, XS)])
     xs.add("h", lambda j: hs.at[trows(j)], lambda j: hr.at[trows(j)], dev_h,
-           lambda j: hr.at[trows(j)])
-
-    def ng_p(j):
-        grads = jnp.concatenate([pg[trows(j)], pg[trows(j, TOK)]], axis=0)
-        for q in range(8):
+           lambda j: hr.at[trows(j)], hs)
+
+    def quarter(i):
+        m, n = i // 2, i % 2
+        return (x + 2 - n + m * (1 - 2 * n)) % 4
+
+    sib = Lane(si_s, si_r)
+    sib.add(
+        "s",
+        lambda i: ng.at[pl.ds(TOK, TOK), span(quarter(i) * XS, XS)],
+        lambda i: nr.at[:, span(quarter(i) * XS, XS)],
+        dev_c,
+        lambda i: nr.at[:, span(quarter(i) * XS, XS)],
+        nr,
+    )
+
+    def grads_times_weight(i, t, lo, n, first):
+        rows = pl.ds(pl.multiple_of((1 - t) * TOK, TOK), TOK)
+        for h in range(2):
+            block = quarter(i) * 2 + h
             part = lax.dot_general(
-                grads, w[q // 4, q % 4], (((1,), (1,)), ((), ())), preferred_element_type=F32
-            ).astype(BF16)
-            ng[trows(j), q * CR : (q + 1) * CR] = part[:TB]
-            ng[trows(j, TOK), q * CR : (q + 1) * CR] = part[TB:]
-        xs.start("sib", j)
-
-    def ng_q(j):
-        xs.arrived("sib", j)
-        ng[trows(j)] = plus(ng[trows(j)], nr[trows(j)]).astype(BF16)
-        xs.start("far_p", j)
-        xs.start("far_m", j)
+                pg[rows, lo : lo + n],
+                w[block // 4, block % 4, :, lo : lo + n],
+                (((1,), (1,)), ((), ())),
+                preferred_element_type=F32,
+            )
+            at = (rows, span(block * CR, CR))
+            ng[at] = part.astype(BF16) if first else plus(part, ng[at]).astype(BF16)
+
+    def ng_first(i):
+        @pl.loop(0, 2)
+        def _(t):
+            grads_times_weight(i, t, 0, KP, True)
+
+    def ng_p(i):
+        @pl.loop(0, 2)
+        def _(t):
+            grads_times_weight(i, t, KP, HALF - KP, False)
+
+            @pl.when(t == 0)
+            def _():
+                sib.start("s", i)
+
+    def ng_q():
+        sib.arrived("s", 0)
+
+        @pl.loop(0, NB)
+        def _(j):
+            at = (trows(j), span(x2 * XS, XS))
+            ng[at] = ng[at] + nr[at]
+            xs.start("far_p", j)
+            xs.start("far_m", j)
+
+    def sibs_here():
+        for i in range(1, 4):
+            sib.arrived("s", i)
 
     def ng_r(j):
+        low, high = (trows(j), span(xp * XS, WS)), (trows(j), span(xp * XS + WS, WS))
         xs.arrived("far_p", j)
-        at = (trows(j), span(xp * XS, WS))
-        ng[at] = plus(ng[at], xf[0, trows(j)]).astype(BF16)
+        ng[low] = ng[low] + nr[low] + xf[0, trows(j)]
+        ng[high] = ng[high] + nr[high]
         xs.start("near_p", j)
+        low, high = (trows(j), span(xm * XS, WS)), (trows(j), span(xm * XS + WS, WS))
         xs.arrived("far_m", j)
-        at = (trows(j), span(xm * XS + WS, WS))
-        ng[at] = plus(ng[at], xf[1, trows(j)]).astype(BF16)
+        ng[high] = ng[high] + nr[high] + xf[1, trows(j)]
+        ng[low] = ng[low] + nr[low]
         xs.start("near_m", j)
 
     def ng_u(j):
@@ -386,15 +429,18 @@
         xs.arrived("near_m", j)
         theirs, ours = span((1 - yh) * WS, WS), span(yh * WS, WS)
         base = x * XS
-        hs[trows(j)] = plus(
-            ng[trows(j), span(base + (1 - yh) * WS, WS)],
-            xn[0, trows(j), theirs],
-            xn[1, trows(j), theirs],
-        ).astype(BF16)
-        xs.start("h", j)
-        ho[trows(j)] = plus(
-            ng[trows(j), span(base + yh * WS, WS)], xn[0, trows(j), ours], xn[1, trows(j), ours]
-        )
+        for half, at in ((theirs, base + (1 - yh) * WS), (ours, base + yh * WS)):
+            total = plus(
+                ng[trows(j), span(at, WS)],
+                nr[trows(j), span(at, WS)],
+                xn[0, trows(j), half],
+                xn[1, trows(j), half],
+            )
+            if half is theirs:
+                hs[trows(j)] = total.astype(BF16)
+                xs.start("h", j)
+            else:
+                ho[trows(j)] = total
 
     def ig_copy(j):
         return pltpu.make_async_copy(igv.at[trows(j)], ig_out.at[trows(j)], ig_sem.at[j])
@@ -410,11 +456,11 @@
         ig_copy(j).start()
 
     rds = Lane(rd_s, rd_r)
-    rds.add("s", lambda k: rdo.at[1], lambda k: rdr, dev_c, lambda k: rdr)
+    rds.add("s", lambda k: rdo.at[1], lambda k: rdr, dev_c, lambda k: rdr, rdr)
     rws = Lane(rw_s, rw_r)
     for r in range(7):
         rws.add(str(r), lambda k: rdo.at[0], lambda k, r=r: rdw.at[r], dev_w[r],
-                lambda k, r=r: rdw.at[r])
+                lambda k, r=r: rdw.at[r], rdr)
 
     def rd_1():
         ones = jnp.ones((8, BLK), F32)
@@ -435,6 +481,7 @@
             rws.start(str(r), 0)
 
     def rd_3():
+        load_tsl.wait()
         for r in range(7):
             rws.arrived(str(r), 0)
         total = rdo[0]
@@ -442,9 +489,7 @@
             total = total + rdw[r]
         rdacc[pl.ds(0, TOK)] = jnp.broadcast_to((total / D).T[:, :1], (TOK, BLK))
 
-    cts.start("c", 0)
     rotation = hadamard()
-    load_cod.wait()
 
     def decoded(core, k):
         at = wide_cols(core, k)
@@ -455,117 +500,112 @@
         low = turned[BLK:] * (grid[codes[1, block]] * norm)
         return jnp.concatenate([top, low], axis=0).astype(BF16)
 
-    @pl.loop(0, CH)
-    def _(k):
+    def decode(k):
         wsib[:, cols(k)] = decoded(1 - c, k)
         swap.start("w", k)
         w[yl, z, mine, cols(k)] = decoded(c, k)
 
-    ag_a(0)
-    ag_a(1)
-    rdacc[...] = jnp.zeros_like(rdacc)
-    load_tok.wait()
-
-    @pl.loop(0, NB)
-    def _(j):
-        @pl.loop(0, TB // 32)
+    @pl.loop(0, CH)
+    def _(k):
+        decode(k)
+        for i in range(LA):
+            @pl.when(k == 2 * i + 2)
+            def _(i=i):
+                ag_a(i)
+
+    cts.start("c", 0)
+
+    def norm_tokens():
+        rdacc[...] = jnp.zeros_like(rdacc)
+        load_tok.wait()
+
+        @pl.loop(0, NB)
+        def _(j):
+            @pl.loop(0, TB // 32)
+            def _(i):
+                rows = pl.ds(pl.multiple_of(j * TB + i * 32, 32), 32)
+                values = ng[rows].astype(F32)
+                scale = lax.rsqrt(
+                    jnp.sum(values * values, axis=-1, keepdims=True) * (1.0 / D) + 1e-5
+                )
+                inv[rows] = jnp.broadcast_to(scale, (32, BLK))
+                normed[rows] = (values * scale * gain[...]).astype(BF16)
+
+            nms.start("n", j)
+
+        load_cot.wait()
+
+    def inputs_here():
+        cts.arrived("c", 0)
+        @pl.loop(0, NB)
+        def _(j):
+            nms.arrived("n", j)
+
+    def at_step(s, fn, first, count, each=1):
+        @pl.when((s >= first) & (s < first + count // each))
+        def _():
+            if each == 1:
+                fn(s - first)
+            else:
+
+                @pl.loop(0, each)
+                def _(i):
+                    fn((s - first) * each + i)
+
+    def once(s, fn, step):
+        @pl.when(s == step)
+        def _():
+            fn()
+
+    def several(fn, k, count):
+        @pl.loop(0, count)
         def _(i):
-            rows = pl.ds(pl.multiple_of(j * TB + i * 32, 32), 32)
-            values = ng[rows].astype(F32)
-            scale = lax.rsqrt(jnp.sum(values * values, axis=-1, keepdims=True) * (1.0 / D) + 1e-5)
-            inv[rows] = jnp.broadcast_to(scale, (32, BLK))
-            normed[rows] = (values * scale * gain[...]).astype(BF16)
-
-        nms.start("n", j)
-
-    @pl.loop(0, CH + 2)
+            fn(k + i)
+
+    done = CH - 1 + LD
+
+    @pl.loop(0, STEPS)
     def _(s):
-        @pl.when(s + 2 < CH)
+        at_step(s, lambda k: ag_a(k + LA), 0, CH - LA)
+        at_step(s, ag_b, 0, CH)
+        at_step(s, ag_c, LC, CH)
+        once(s, norm_tokens, 0)
+        once(s, inputs_here, LD)
+        once(s, lambda: several(rs_a, 0, 4), CH)
+        once(s, lambda: several(weight_part, 4, 3), done + 1)
+        once(s, lambda: several(rs_a, 4, 3), done + 1)
+        at_step(s, lambda k: rs_b(k + 2), done + 1, CH - 2)
+        once(s, sibs_here, done + NR)
+        at_step(s, ng_r, done + NR, NB, ER)
+        at_step(s, rs_c, done + RC, CH)
+        at_step(s, ng_u, done + NU, NB, EU)
+        once(s, rd_1, done + 2)
+        once(s, rd_2, done + 3)
+        once(s, rd_3, done + 4)
+        at_step(s, ng_v, done + NV, NB, EU)
+        at_step(s, rs_d, done + RD, CH)
+        once(s, lambda: several(weight_part, 0, 2), LD + 2)
+        once(s, lambda: several(weight_part, 2, 2), LD + 4)
+        at_step(s, ng_first, LD + 4, 4, 2)
+        at_step(s, ag_d, LD, CH)
+
+        @pl.when((s > LD) & (s < done) & ((s - LD) % 2 == 1))
         def _():
-            ag_a(s + 2)
-
-        @pl.when(s < CH)
+            forward(s - LD - 1, 2)
+
+        once(s, lambda: forward(CH - 1, 1), done)
+
+        @pl.when(s == done)
         def _():
-            ag_b(s)
-
-        @pl.when((s >= 1) & (s < CH + 1))
-        def _():
-            ag_c(s - 1)
-
-        @pl.when(s >= CH)
-        def _():
-            rs_a(s - CH)
-
-        @pl.when(s == 2)
-        def _():
-            load_cot.wait()
-            cts.arrived("c", 0)
-            for j in range(NB):
-                nms.arrived("n", j)
-
-        @pl.when(s >= 2)
-        def _():
-            ag_d(s - 2)
-            compute(s - 2)
-
-    rd_1()
-
-    @pl.loop(0, CH + 2)
-    def _(t):
-        @pl.when(t + 2 < CH)
-        def _():
-            rs_a(t + 2)
-
-        @pl.when(t < NB)
-        def _():
-            ng_p(t)
-
-        @pl.when(t < CH)
-        def _():
-            rs_b(t)
-
-        @pl.when(t < NB)
-        def _():
-            ng_q(t)
-
-        @pl.when((t >= 1) & (t < CH + 1))
-        def _():
-            rs_c(t - 1)
-
-        @pl.when(t == 1)
-        def _():
-            rd_2()
-
-        @pl.when((t >= 2) & (t < NB + 2))
-        def _():
-            ng_r(t - 2)
-
-        @pl.when(t >= 2)
-        def _():
-            rs_d(t - 2)
-
-        @pl.when(t == 3)
-        def _():
-            load_tsl.wait()
-            rd_3()
-
-        @pl.when((t >= 4) & (t < NB + 4))
-        def _():
-            ng_u(t - 4)
-
-        @pl.when((t >= 5) & (t < NB + 5))
-        def _():
-            ng_v(t - 5)
-
-    swap.drain(CH)
-    ag.drain(CH)
-    rs.drain(CH)
-    nms.drain(NB)
-    xs.drain(NB)
-    cts.sent("c", 0)
-    rds.sent("s", 0)
-    for r in range(7):
-        rws.sent(str(r), 0)
+            @pl.loop(0, 2)
+            def _(i):
+                rs_b(i)
+                several(ng_p, 2 * i, 2)
+
+            ng_q()
+
+    for lane in (swap, ag, rs, nms, xs, sib, cts, rds, rws):
+        lane.drain()
 
     @pl.loop(0, CH)
     def _(k):
@@ -625,10 +665,9 @@
             pltpu.VMEM((2, CH, R1, BLK), BF16),
             pltpu.VMEM((CH, R2, BLK), BF16),
             sem((4,)), sem((3, CH)), sem((3, CH)), sem((NB,)),
-            sem((12, CH)), sem((12, CH)), sem((10, CH)), sem((10, CH)),
-            sem((1, CH)), sem((1, CH)), sem((1, NB)), sem((1, NB)),
-            sem((6, NB)), sem((6, NB)), sem((1, 1)), sem((1, 1)),
-            sem((7, 1)), sem((7, 1)), sem((1, 1)), sem((1, 1)),
+            sem((12,)), sem((12, CH)), sem((10,)), sem((10, CH)), sem((1,)), sem((1, 4)),
+            sem((1,)), sem((1, CH)), sem((1,)), sem((1, NB)), sem((5,)), sem((5, NB)),
+            sem((1,)), sem((1, 1)), sem((7,)), sem((7, 1)), sem((1,)), sem((1, 1)),
         ],
         compiler_params=pltpu.CompilerParams(
             collective_id=0, has_side_effects=True, vmem_limit_bytes=63 << 20

time: 132 us -> 130 us (0.985)
  Pallas kernels: 126 us -> 124 us
    pallas_call x1, Pallas kernels: 126 us -> 124 us  [per_device(): pl.pallas_call(kernel, out_shape=(jax.ShapeDtypeStruct((TOK, CW), BF16),...]
where the time goes in v2:
time: 130 us
  Pallas kernels  124 us (95%)
  local copies, waits for them, and re-layouts  5.17 us (4%)
    pallas_call x1, Pallas kernels, per_device(): pl.pallas_call(kernel, out_shape=(jax.ShapeDtypeStruct((TOK, CW), BF16),...  124 us
    unnamed x7, local copies, waits for them, and re-layouts  5.17 us

profile of v2, /device:TPU:1, one launch (start us, length us, event | category | flops | bytes accessed | tf_op | source)
XLA Modules:
  0.0 130.0 jit_solution(8299327375334591084)
XLA Ops:
  0.6 124.2 %shard_map.85 = (bf16[512,1792]{1,0:T(8,128)(2,1)}, f32[256,1792]{1,0:T(8,128)}, bf16[512,512]{1,0:T(8,128)(2,1)}) custom-call(bf16[512,4096]{1,0:T(8,128)(2,1)} %tokens.1, f32[1,4096]{1,0:T(1,128)} %bitcast.1, bf16[256,1792]{1,0:T(8,128)(2,1)} %coded.1, s32[2,14]{1,0:T(2,128)} %codes.1, f32[16]{0:T(128)} %grid.1, bf16[512,1792]{1,0:T(8,128)(2,1)} %cot.1), custom_call_target="tpu_custom_call" | custom-call | flops 22548578304 | bytes 41943040 | tf_op jit(solution)/shard_map/pallas_call | solution.py:629
  124.8 0.0 copy-start
  124.8 3.0 %copy.12 = bf16[512,1792]{1,0:T(8,128)(2,1)} copy(bf16[512,1792]{1,0:T(8,128)(2,1)} %get-tuple-element.6) | data formatting | bytes 3670016
  127.8 0.0 copy-done
  127.8 0.0 copy-start.1
  127.8 1.2 copy.13
  129.0 0.2 copy-done.1
  129.2 0.8 copy.14
Async XLA Ops:
  124.8 3.0 %copy-start = (f32[256,1792]{1,0:T(8,128)S(1)}, f32[256,1792]{1,0:T(8,128)}, u32[]{:S(2)}) copy-start(f32[256,1792]{1,0:T(8,128)} %get-tuple-element.7) | copy-start | bytes 5505028
  127.8 1.4 %copy-start.1 = (bf16[512,512]{1,0:T(8,128)(2,1)S(1)}, bf16[512,512]{1,0:T(8,128)(2,1)}, u32[]{:S(2)}) copy-start(bf16[512,512]{1,0:T(8,128)(2,1)} %get-tuple-element.8) | copy-start | bytes 1572868

commit v3 on v2

--- a/solution.py
+++ b/solution.py
@@ -28,8 +28,10 @@
 
 LA, LC, LD = 1, 1, 2
 RC, RD = 1, 3
-NR, NU, NV = 2, 4, 5
+RE = 1
+NR, NU, NV = 2, 3, 5
 ER, EU = 2, 2
+PARTS = 2
 STEPS = CH - 1 + LD + max(CH + RD, NV + NB // EU)
 
 
@@ -161,18 +163,22 @@
     ag = Lane(ag_s, ag_r)
 
     def piece(name, device, src_at, land_at, lo, n):
+        piece_of(name, device, src_at, land_at, pl.ds(lo, n))
+
+    def piece_of(name, device, src_at, land_at, rows):
         ag.add(
             name,
-            lambda k: w.at[src_at[0], src_at[1], pl.ds(lo, n), cols(k)],
-            lambda k: w.at[src_at[0], src_at[1], pl.ds(lo, n), cols(k)],
+            lambda k: w.at[src_at[0], src_at[1], rows, cols(k)],
+            lambda k: w.at[src_at[0], src_at[1], rows, cols(k)],
             device,
-            lambda k: w.at[land_at[0], land_at[1], pl.ds(lo, n), cols(k)],
-            w.at[src_at[0], src_at[1], pl.ds(lo, n)],
+            lambda k: w.at[land_at[0], land_at[1], rows, cols(k)],
+            w.at[src_at[0], src_at[1], rows],
         )
 
-    piece("own_zp", dev_zp, (yl, z), (yl, zm), 0, CR)
-    piece("own_zm", dev_zm, (yl, z), (yl, zp), 0, CR)
-    piece("own_y", dev_y, (yl, z), (yo, z), 0, CR)
+    for half, rows in (("mine", mine), ("other", other)):
+        piece_of("zp_" + half, dev_zp, (yl, z), (yl, zm), rows)
+        piece_of("zm_" + half, dev_zm, (yl, z), (yl, zp), rows)
+        piece_of("y_" + half, dev_y, (yl, z), (yo, z), rows)
     piece("far_zp", dev_zp, (yl, zm), (yl, z2), 0, CR // 2)
     piece("far_zm", dev_zm, (yl, zp), (yl, z2), CR // 2, CR // 2)
     piece("zm_y", dev_y, (yl, zm), (yo, zm), 0, G1)
@@ -183,20 +189,27 @@
     piece("yfar_zp", dev_zp, (yo, zm), (yo, z2), G1, GH)
     piece("yfar_zm", dev_zm, (yo, zp), (yo, z2), G1 + GH, GH)
 
+    def ag_own(k, half):
+        ag.start("zp_" + half, k)
+        ag.start("zm_" + half, k)
+        ag.start("y_" + half, k)
+
     def ag_a(k):
+        ag_own(k, "mine")
         swap.arrived("w", k)
-        ag.start("own_zp", k)
-        ag.start("own_zm", k)
-        ag.start("own_y", k)
+        ag_own(k, "other")
 
     def ag_b(k):
-        ag.arrived("own_y", k)
+        ag.arrived("y_mine", k)
+        ag.arrived("y_other", k)
         ag.start("y_zp", k)
         ag.start("y_zm", k)
-        ag.arrived("own_zp", k)
+        ag.arrived("zp_mine", k)
+        ag.arrived("zp_other", k)
         ag.start("far_zp", k)
         ag.start("zm_y", k)
-        ag.arrived("own_zm", k)
+        ag.arrived("zm_mine", k)
+        ag.arrived("zm_other", k)
         ag.start("far_zm", k)
         ag.start("zp_y", k)
 
@@ -505,13 +518,17 @@
         swap.start("w", k)
         w[yl, z, mine, cols(k)] = decoded(c, k)
 
-    @pl.loop(0, CH)
+    decode(0)
+    ag_own(0, "mine")
+
+    @pl.loop(1, CH)
     def _(k):
         decode(k)
-        for i in range(LA):
-            @pl.when(k == 2 * i + 2)
-            def _(i=i):
-                ag_a(i)
+
+    swap.arrived("w", 0)
+    ag_own(0, "other")
+    for i in range(1, LA):
+        ag_a(i)
 
     cts.start("c", 0)
 
@@ -571,7 +588,8 @@
         at_step(s, ag_c, LC, CH)
         once(s, norm_tokens, 0)
         once(s, inputs_here, LD)
-        once(s, lambda: several(rs_a, 0, 4), CH)
+        once(s, lambda: several(rs_a, 0, RE), CH - 1)
+        once(s, lambda: several(rs_a, RE, 4 - RE), CH)
         once(s, lambda: several(weight_part, 4, 3), done + 1)
         once(s, lambda: several(rs_a, 4, 3), done + 1)
         at_step(s, lambda k: rs_b(k + 2), done + 1, CH - 2)
@@ -621,12 +639,31 @@
         ig_copy(j).wait()
 
 
+def hand_over(act, wg, ig, act_out, wg_out, ig_out, act_v, wg_v, ig_v, sems):
+    loads, stores = [], []
+    for i, (src, mid, dst) in enumerate(
+        ((act, act_v, act_out), (wg, wg_v, wg_out), (ig, ig_v, ig_out))
+    ):
+        rows = src.shape[0] // PARTS
+        for part in range(PARTS):
+            at = pl.ds(part * rows, rows)
+            loads.append(pltpu.make_async_copy(src.at[at], mid.at[at], sems.at[0, i, part]))
+            stores.append(pltpu.make_async_copy(mid.at[at], dst.at[at], sems.at[1, i, part]))
+    for load in loads:
+        load.start()
+    for load, store in zip(loads, stores):
+        load.wait()
+        store.start()
+    for store in stores:
+        store.wait()
+
+
 def per_device(tokens, norm_gain, coded, block_codes, grid, cotangent):
     anywhere = pl.BlockSpec(memory_space=pl.ANY)
     vmem = pl.BlockSpec(memory_space=pltpu.VMEM)
     smem = pl.BlockSpec(memory_space=pltpu.SMEM)
     sem = pltpu.SemaphoreType.DMA
-    return pl.pallas_call(
+    results = pl.pallas_call(
         kernel,
         out_shape=(
             jax.ShapeDtypeStruct((TOK, CW), BF16),
@@ -665,7 +702,7 @@
             pltpu.VMEM((2, CH, R1, BLK), BF16),
             pltpu.VMEM((CH, R2, BLK), BF16),
             sem((4,)), sem((3, CH)), sem((3, CH)), sem((NB,)),
-            sem((12,)), sem((12, CH)), sem((10,)), sem((10, CH)), sem((1,)), sem((1, 4)),
+            sem((15,)), sem((15, CH)), sem((10,)), sem((10, CH)), sem((1,)), sem((1, 4)),
             sem((1,)), sem((1, CH)), sem((1,)), sem((1, NB)), sem((5,)), sem((5, NB)),
             sem((1,)), sem((1, 1)), sem((7,)), sem((7, 1)), sem((1,)), sem((1, 1)),
         ],
@@ -676,6 +713,14 @@
             flops=6 * TOK * D * CW, bytes_accessed=40 << 20, transcendentals=TOK * CW
         ),
     )(tokens, norm_gain.reshape(1, D), coded, block_codes, grid, cotangent)
+    return pl.pallas_call(
+        hand_over,
+        out_shape=tuple(jax.ShapeDtypeStruct(r.shape, r.dtype) for r in results),
+        in_specs=[anywhere] * 3,
+        out_specs=(anywhere,) * 3,
+        scratch_shapes=[pltpu.VMEM(r.shape, r.dtype) for r in results] + [sem((2, 3, PARTS))],
+        compiler_params=pltpu.CompilerParams(vmem_limit_bytes=63 << 20),
+    )(*results)
 
 
 def solution(mesh):

time: 130 us -> 126 us (0.969)
  local copies, waits for them, and re-layouts: 5.17 us -> 0 us
    unnamed x7 -> x0, local copies, waits for them, and re-layouts: 5.17 us -> none
    pallas_call x0 -> x1, Pallas kernels: none -> 3.28 us  [per_device(): pl.pallas_call(hand_over, out_shape=tuple((jax.ShapeDtypeStruct(r.shape,...]
    pallas_call x1, Pallas kernels: 124 us -> 122 us  [per_device(): pl.pallas_call(kernel, out_shape=(jax.ShapeDtypeStruct((TOK, CW), BF16),...]
where the time goes in v3:
time: 126 us
  Pallas kernels  125 us (99%)
    pallas_call x1, Pallas kernels, per_device(): pl.pallas_call(kernel, out_shape=(jax.ShapeDtypeStruct((TOK, CW), BF16),...  122 us
    pallas_call x1, Pallas kernels, per_device(): pl.pallas_call(hand_over, out_shape=tuple((jax.ShapeDtypeStruct(r.shape,...  3.28 us

profile of v3, /device:TPU:1, one launch (start us, length us, event | category | flops | bytes accessed | tf_op | source)
XLA Modules:
  0.0 125.7 jit_solution(9297218839637206911)
XLA Ops:
  0.6 121.8 %shard_map.85 = (bf16[512,1792]{1,0:T(8,128)(2,1)}, f32[256,1792]{1,0:T(8,128)}, bf16[512,512]{1,0:T(8,128)(2,1)}) custom-call(bf16[512,4096]{1,0:T(8,128)(2,1)} %tokens.1, f32[1,4096]{1,0:T(1,128)} %bitcast.1, bf16[256,1792]{1,0:T(8,128)(2,1)} %coded.1, s32[2,14]{1,0:T(2,128)} %codes.1, f32[16]{0:T(128)} %grid.1, bf16[512,1792]{1,0:T(8,128)(2,1)} %cot.1), custom_call_target="tpu_custom_call" | custom-call | flops 22548578304 | bytes 41943040 | tf_op jit(solution)/shard_map/pallas_call | solution.py:666
  122.4 3.3 %shard_map.86 = (bf16[512,1792]{1,0:T(8,128)(2,1)}, f32[256,1792]{1,0:T(8,128)}, bf16[512,512]{1,0:T(8,128)(2,1)}) custom-call(bf16[512,1792]{1,0:T(8,128)(2,1)} %get-tuple-element.6.act, f32[256,1792]{1,0:T(8,128)} %get-tuple-element.7.wg, bf16[512,512]{1,0:T(8,128)(2,1)} %get-tuple-element.8.ig), custom_call_target="tpu_custom_call" | custom-call | tf_op jit(solution)/shard_map/pallas_call | solution.py:716

commit v4 on v3

--- a/solution.py
+++ b/solution.py
@@ -590,7 +590,7 @@
         once(s, inputs_here, LD)
         once(s, lambda: several(rs_a, 0, RE), CH - 1)
         once(s, lambda: several(rs_a, RE, 4 - RE), CH)
-        once(s, lambda: several(weight_part, 4, 3), done + 1)
+        once(s, lambda: several(weight_part, 5, 2), done + 1)
         once(s, lambda: several(rs_a, 4, 3), done + 1)
         at_step(s, lambda k: rs_b(k + 2), done + 1, CH - 2)
         once(s, sibs_here, done + NR)
@@ -604,13 +604,14 @@
         at_step(s, rs_d, done + RD, CH)
         once(s, lambda: several(weight_part, 0, 2), LD + 2)
         once(s, lambda: several(weight_part, 2, 2), LD + 4)
-        at_step(s, ng_first, LD + 4, 4, 2)
         at_step(s, ag_d, LD, CH)
 
         @pl.when((s > LD) & (s < done) & ((s - LD) % 2 == 1))
         def _():
             forward(s - LD - 1, 2)
 
+        at_step(s, ng_first, LD + 3, 4, 2)
+        once(s, lambda: weight_part(4), CH)
         once(s, lambda: forward(CH - 1, 1), done)
 
         @pl.when(s == done)

time: 126 us -> 124 us (0.984)
    pallas_call x1, Pallas kernels: 122 us -> 120 us  [per_device(): pl.pallas_call(kernel, out_shape=(jax.ShapeDtypeStruct((TOK, CW), BF16),...]
where the time goes in v4:
time: 124 us
  Pallas kernels  124 us (100%)
    pallas_call x1, Pallas kernels, per_device(): pl.pallas_call(kernel, out_shape=(jax.ShapeDtypeStruct((TOK, CW), BF16),...  120 us
    pallas_call x1, Pallas kernels, per_device(): pl.pallas_call(hand_over, out_shape=tuple((jax.ShapeDtypeStruct(r.shape,...  3.28 us

profile of v4, /device:TPU:1, one launch (start us, length us, event | category | flops | bytes accessed | tf_op | source)
XLA Modules:
  0.0 124.3 jit_solution(7696068432725247494)
XLA Ops:
  0.6 120.4 %shard_map.85 = (bf16[512,1792]{1,0:T(8,128)(2,1)}, f32[256,1792]{1,0:T(8,128)}, bf16[512,512]{1,0:T(8,128)(2,1)}) custom-call(bf16[512,4096]{1,0:T(8,128)(2,1)} %tokens.1, f32[1,4096]{1,0:T(1,128)} %bitcast.1, bf16[256,1792]{1,0:T(8,128)(2,1)} %coded.1, s32[2,14]{1,0:T(2,128)} %codes.1, f32[16]{0:T(128)} %grid.1, bf16[512,1792]{1,0:T(8,128)(2,1)} %cot.1), custom_call_target="tpu_custom_call" | custom-call | flops 22548578304 | bytes 41943040 | tf_op jit(solution)/shard_map/pallas_call | solution.py:667
  121.0 3.3 %shard_map.86 = (bf16[512,1792]{1,0:T(8,128)(2,1)}, f32[256,1792]{1,0:T(8,128)}, bf16[512,512]{1,0:T(8,128)(2,1)}) custom-call(bf16[512,1792]{1,0:T(8,128)(2,1)} %get-tuple-element.6.act, f32[256,1792]{1,0:T(8,128)} %get-tuple-element.7.wg, bf16[512,512]{1,0:T(8,128)(2,1)} %get-tuple-element.8.ig), custom_call_target="tpu_custom_call" | custom-call | tf_op jit(solution)/shard_map/pallas_call | solution.py:717

commit v5 on v4

--- a/solution.py
+++ b/solution.py
@@ -590,7 +590,7 @@
         once(s, inputs_here, LD)
         once(s, lambda: several(rs_a, 0, RE), CH - 1)
         once(s, lambda: several(rs_a, RE, 4 - RE), CH)
-        once(s, lambda: several(weight_part, 5, 2), done + 1)
+        once(s, lambda: weight_part(6), done + 1)
         once(s, lambda: several(rs_a, 4, 3), done + 1)
         at_step(s, lambda k: rs_b(k + 2), done + 1, CH - 2)
         once(s, sibs_here, done + NR)
@@ -604,6 +604,7 @@
         at_step(s, rs_d, done + RD, CH)
         once(s, lambda: several(weight_part, 0, 2), LD + 2)
         once(s, lambda: several(weight_part, 2, 2), LD + 4)
+        once(s, lambda: weight_part(5), done)
         at_step(s, ag_d, LD, CH)
 
         @pl.when((s > LD) & (s < done) & ((s - LD) % 2 == 1))

time: 124 us -> 126 us (1.016)
    pallas_call x1, Pallas kernels: 120 us -> 122 us  [per_device(): pl.pallas_call(kernel, out_shape=(jax.ShapeDtypeStruct((TOK, CW), BF16),...]
where the time goes in v5:
time: 126 us
  Pallas kernels  125 us (99%)
    pallas_call x1, Pallas kernels, per_device(): pl.pallas_call(kernel, out_shape=(jax.ShapeDtypeStruct((TOK, CW), BF16),...  122 us
    pallas_call x1, Pallas kernels, per_device(): pl.pallas_call(hand_over, out_shape=tuple((jax.ShapeDtypeStruct(r.shape,...  3.28 us

profile of v5, /device:TPU:1, one launch (start us, length us, event | category | flops | bytes accessed | tf_op | source)
XLA Modules:
  0.0 125.7 jit_solution(14612826563723345026)
XLA Ops:
  0.6 121.8 %shard_map.85 = (bf16[512,1792]{1,0:T(8,128)(2,1)}, f32[256,1792]{1,0:T(8,128)}, bf16[512,512]{1,0:T(8,128)(2,1)}) custom-call(bf16[512,4096]{1,0:T(8,128)(2,1)} %tokens.1, f32[1,4096]{1,0:T(1,128)} %bitcast.1, bf16[256,1792]{1,0:T(8,128)(2,1)} %coded.1, s32[2,14]{1,0:T(2,128)} %codes.1, f32[16]{0:T(128)} %grid.1, bf16[512,1792]{1,0:T(8,128)(2,1)} %cot.1), custom_call_target="tpu_custom_call" | custom-call | flops 22548578304 | bytes 41943040 | tf_op jit(solution)/shard_map/pallas_call | solution.py:668
  122.4 3.3 %shard_map.86 = (bf16[512,1792]{1,0:T(8,128)(2,1)}, f32[256,1792]{1,0:T(8,128)}, bf16[512,512]{1,0:T(8,128)(2,1)}) custom-call(bf16[512,1792]{1,0:T(8,128)(2,1)} %get-tuple-element.6.act, f32[256,1792]{1,0:T(8,128)} %get-tuple-element.7.wg, bf16[512,512]{1,0:T(8,128)(2,1)} %get-tuple-element.8.ig), custom_call_target="tpu_custom_call" | custom-call | tf_op jit(solution)/shard_map/pallas_call | solution.py:718
